TPU v7x, 32 devices: a whole 2x2x4 slice. The times are simulated.
32 devices in a mesh: head: 4 (over x, core), batch: 8 (over z, y).
Axes of the slice: x: 2, y: 2, z: 4, core: 2. Of those that a mesh axis runs over, the one named last changes fastest.
Arguments:
- content: bfloat16 [8, 512, 768], P('batch', 'head'), may hold values from -6 to 6
- query_stream: bfloat16 [8, 96, 768], P('batch', 'head'), may hold values from -6 to 6
- memory: bfloat16 [8, 384, 768], P('batch', 'head'), may hold values from -6 to 6
- has_memory: int32 [8], P('batch'), may hold values 0 or 1
- order_rank: int32 [8, 512], P('batch'), may hold values from 0 to 511, as said below
- targets: int32 [8, 96], P('batch'), may hold values from 0 to 511, as said below
- segments: int32 [8, 512], P('batch'), may hold values from 0 to 1, never falling along the last dimension, each value on 1 to 384 neighbouring positions
- query_weight: bfloat16 [768, 768], P(None, 'head'), may hold values from -0.21875 to 0.21875
- key_weight: bfloat16 [768, 768], P(None, 'head'), may hold values from -0.21875 to 0.21875
- value_weight: bfloat16 [768, 768], P(None, 'head'), may hold values from -0.21875 to 0.21875
- output_weight: bfloat16 [768, 768], P('head'), may hold values from -3.5 to 3.5
- relative_weight: bfloat16 [768, 768], P(None, 'head'), may hold values from -0.21875 to 0.21875
- word_bias: bfloat16 [12, 64], P('head'), may hold values from -3 to 3
- position_bias: bfloat16 [12, 64], P('head'), may hold values from -3 to 3
- segment_bias: bfloat16 [12, 64], P('head'), may hold values from -3 to 3
- segment_embed: bfloat16 [2, 12, 64], P(None, 'head'), may hold values from -3 to 3
- first_gain: bfloat16 [768], replicated, may hold values from 0.5 to 1.5
- first_shift: bfloat16 [768], replicated, may hold values from -2 to 2
- inner_weight: bfloat16 [768, 3072], P(None, 'head'), may hold values from -0.21875 to 0.21875
- inner_bias: bfloat16 [3072], P('head'), may hold values from -2 to 2
- outer_weight: bfloat16 [3072, 768], P('head'), may hold values from -0.109375 to 0.109375
- outer_bias: bfloat16 [768], replicated, may hold values from -2 to 2
- second_gain: bfloat16 [768], replicated, may hold values from 0.5 to 1.5
- second_shift: bfloat16 [768], replicated, may hold values from -2 to 2
- content_cotangent: bfloat16 [8, 512, 768], P('batch', 'head'), may hold values from -6 to 6
- query_cotangent: bfloat16 [8, 96, 768], P('batch', 'head'), may hold values from -6 to 6
Outputs:
- content_out: bfloat16 [8, 512, 768], P('batch', 'head')
- query_out: bfloat16 [8, 96, 768], P('batch', 'head')
- content_grad: float32 [8, 512, 768], P('batch', 'head')
- query_grad: float32 [8, 96, 768], P('batch', 'head')
- query_weight_grad: float32 [768, 768], P(None, 'head')
- key_weight_grad: float32 [768, 768], P(None, 'head')
- value_weight_grad: float32 [768, 768], P(None, 'head')
- output_weight_grad: float32 [768, 768], P('head')
- relative_weight_grad: float32 [768, 768], P(None, 'head')
- word_bias_grad: float32 [12, 64], P('head')
- position_bias_grad: float32 [12, 64], P('head')
- segment_bias_grad: float32 [12, 64], P('head')
- segment_embed_grad: float32 [2, 12, 64], P(None, 'head')
- first_gain_grad: float32 [768], replicated
- first_shift_grad: float32 [768], replicated
- inner_weight_grad: float32 [768, 3072], P(None, 'head')
- inner_bias_grad: float32 [3072], P('head')
- outer_weight_grad: float32 [3072, 768], P('head')
- outer_bias_grad: float32 [768], replicated
- second_gain_grad: float32 [768], replicated
- second_shift_grad: float32 [768], replicated
Inputs may be any that keep to these rules, and one draw needn't show every extreme that they name: `order_rank`: each row is a permutation of 0 to 511. `targets`: each row lists in ascending order the 96 positions whose order_rank is 416 or more. `segments`: never falling along a row.
All inputs are finite; a program needn't handle non-finite values. No bound on the sum of `has_memory` on one device may be relied on, other than what follows from the above.
Results may differ from a plain program's by a relative error of at most 0.023.
Values may be sent and summed in bfloat16 or wider, within the bound.
No kernel may reach another device: no remote copies, remote signals or barrier semaphores. Data moves between devices by JAX's collectives and lax.ppermute only.
A program may use at most 320 MiB of HBM per device.

v0:
```python
import jax
import jax.numpy as jnp
from jax import lax
from jax.sharding import PartitionSpec as P

highest = lax.Precision.HIGHEST
score_scale = 0.125
masked_score = -1e30
norm_eps = 1e-05
gelu_root = 0.7978845608028654
gelu_cubic = 0.044715


def layer_norm(values, gain, shift):
    center = values - jnp.mean(values, axis=-1, keepdims=True)
    spread = jnp.mean(center * center, axis=-1, keepdims=True)
    return center * lax.rsqrt(spread + norm_eps) * gain + shift


def gelu_tanh(values):
    return (
        0.5
        * values
        * (1.0 + jnp.tanh(gelu_root * (values + gelu_cubic * values * values * values)))
    )


def positions(key_count, length, width):
    steps = jnp.arange(key_count, -length, -1).astype(jnp.float32)
    freqs = 1.0 / 10000.0 ** (jnp.arange(0, width, 2).astype(jnp.float32) / width)
    angles = steps[:, None] * freqs[None, :]
    return jnp.concatenate([jnp.sin(angles), jnp.cos(angles)], axis=1)


def shift_rows(scores):
    heads, length, total = scores.shape
    return scores.reshape(heads, total, length)[:, 1:].reshape(heads, length, total - 1)[
        :, :, : total - length
    ]


def unshift_rows(grads, total):
    heads, length, key_count = grads.shape
    padded = jnp.pad(grads, ((0, 0), (0, 0), (0, total - 1 - key_count)))
    flat = padded.reshape(heads, length * (total - 1))
    return jnp.concatenate([jnp.zeros((heads, length), grads.dtype), flat], axis=1).reshape(
        heads, length, total
    )


def slide_rows(scores, offsets, width):

    def slide_one_row(row, start):
        return lax.dynamic_slice_in_dim(row, start, width)

    return jax.vmap(jax.vmap(slide_one_row), in_axes=(0, None))(scores, offsets)


def unslide_rows(grads, offsets, total):

    def unslide_one_row(row, start):
        return lax.dynamic_update_slice_in_dim(jnp.zeros((total,), row.dtype), row, start, 0)

    return jax.vmap(jax.vmap(unslide_one_row), in_axes=(0, None))(grads, offsets)


def masks(present, ranks, picks, labels, memory_rows):
    length = ranks.shape[0]
    picked = picks[:, None] == jnp.arange(length, dtype=jnp.int32)[None, :]
    pick_rank = jnp.sum(jnp.where(picked, ranks[None, :], 0), axis=1)
    pick_label = jnp.sum(jnp.where(picked, labels[None, :], 0), axis=1)
    limit = jnp.concatenate([ranks + 1, pick_rank])
    key_rank = jnp.concatenate([jnp.full((memory_rows,), -1, jnp.int32), ranks])
    is_memory = jnp.arange(memory_rows + length, dtype=jnp.int32) < memory_rows
    visible = jnp.where(is_memory[None, :], present > 0, key_rank[None, :] < limit[:, None])
    row_label = jnp.concatenate([labels, pick_label])
    key_label = jnp.concatenate([jnp.zeros((memory_rows,), jnp.int32), labels])
    differ = row_label[:, None] != key_label[None, :]
    offsets = length - picks
    return (visible, differ, offsets)


def on_device(
    content,
    query_stream,
    memory,
    has_memory,
    order_rank,
    targets,
    segments,
    query_weight,
    key_weight,
    value_weight,
    output_weight,
    relative_weight,
    word_bias,
    position_bias,
    segment_bias,
    segment_embed,
    first_gain,
    first_shift,
    inner_weight,
    inner_bias,
    outer_weight,
    outer_bias,
    second_gain,
    second_shift,
    content_cotangent,
    query_cotangent,
):
    full_content, full_query, full_memory = (
        lax.all_gather(content, "head", axis=1, tiled=True),
        lax.all_gather(query_stream, "head", axis=1, tiled=True),
        lax.all_gather(memory, "head", axis=1, tiled=True),
    )
    seq_count, length, width = full_content.shape
    memory_rows = full_memory.shape[1]
    key_count = memory_rows + length
    table_rows = key_count + length
    heads, head_size = word_bias.shape
    local_width = heads * head_size
    position_table = positions(key_count, length, width).astype(jnp.bfloat16)
    relative_keys = (
        jnp.dot(position_table, relative_weight, preferred_element_type=jnp.float32)
        .astype(jnp.bfloat16)
        .reshape(table_rows, heads, head_size)
    )
    word_shift = word_bias.astype(jnp.float32)
    place_shift = position_bias.astype(jnp.float32)
    label_shift = segment_bias.astype(jnp.float32)
    segment_table = segment_embed.astype(jnp.float32)
    stream_rows = jnp.concatenate([full_content, full_query], axis=1)
    joined_rows = jnp.concatenate([full_memory, full_content], axis=1)
    row_count = stream_rows.shape[1]

    def score_block(stream, joined, present, ranks, picks, labels):
        visible, differ, offsets = masks(present, ranks, picks, labels, memory_rows)
        query_full = jnp.dot(stream, query_weight, preferred_element_type=jnp.float32).reshape(
            row_count, heads, head_size
        )
        query_word = (query_full + word_shift).astype(jnp.bfloat16)
        query_place = (query_full + place_shift).astype(jnp.bfloat16)
        query_label = query_full + label_shift
        keys = (
            jnp.dot(joined, key_weight, preferred_element_type=jnp.float32)
            .astype(jnp.bfloat16)
            .reshape(key_count, heads, head_size)
        )
        values = (
            jnp.dot(joined, value_weight, preferred_element_type=jnp.float32)
            .astype(jnp.bfloat16)
            .reshape(key_count, heads, head_size)
        )
        content_term = jnp.einsum(
            "ihd,jhd->hij", query_word, keys, preferred_element_type=jnp.float32
        )
        relative_all = jnp.einsum(
            "ihd,rhd->hir", query_place, relative_keys, preferred_element_type=jnp.float32
        )
        place_term = jnp.concatenate(
            [
                shift_rows(relative_all[:, :length]),
                slide_rows(relative_all[:, length:], offsets, key_count),
            ],
            axis=1,
        )
        label_same = jnp.einsum("ihd,hd->hi", query_label, segment_table[0], precision=highest)
        label_other = jnp.einsum("ihd,hd->hi", query_label, segment_table[1], precision=highest)
        label_term = jnp.where(differ[None], label_other[:, :, None], label_same[:, :, None])
        scores = jnp.where(
            visible[None], (content_term + place_term + label_term) * score_scale, masked_score
        )
        return (
            scores,
            visible,
            differ,
            offsets,
            query_word,
            query_place,
            query_label,
            keys,
            values,
        )

    def attend_forward(inputs):
        block = score_block(*inputs)
        scores = block[0]
        row_max = jnp.max(scores, axis=-1, keepdims=True)
        powers = jnp.exp(scores - row_max)
        total = jnp.sum(powers, axis=-1, keepdims=True)
        soft_weights = (powers / total).astype(jnp.bfloat16)
        attended = (
            jnp.einsum("hij,jhd->ihd", soft_weights, block[8], preferred_element_type=jnp.float32)
            .astype(jnp.bfloat16)
            .reshape(row_count, local_width)
        )
        partial_out = jnp.dot(attended, output_weight, preferred_element_type=jnp.float32)
        return (partial_out, (row_max + jnp.log(total))[:, :, 0])

    partials, log_totals = lax.map(
        attend_forward, (stream_rows, joined_rows, has_memory, order_rank, targets, segments)
    )
    attention_content, attention_query = (
        lax.psum_scatter(partials[:, :length], "head", scatter_dimension=1, tiled=True),
        lax.psum_scatter(partials[:, length:], "head", scatter_dimension=1, tiled=True),
    )
    split_at = content.shape[1]
    local_rows = jnp.concatenate([content, query_stream], axis=1).astype(jnp.float32)
    mixed = (local_rows + jnp.concatenate([attention_content, attention_query], axis=1)).reshape(
        -1, width
    )
    hidden, first_back = jax.vjp(
        layer_norm, mixed, first_gain.astype(jnp.float32), first_shift.astype(jnp.float32)
    )
    hidden_low = hidden.astype(jnp.bfloat16)
    inner_used, inner_shift, outer_used = (
        lax.all_gather(inner_weight, "head", axis=1, tiled=True),
        lax.all_gather(inner_bias, "head", axis=0, tiled=True),
        lax.all_gather(outer_weight, "head", axis=0, tiled=True),
    )
    inner = jnp.dot(
        hidden_low, inner_used, preferred_element_type=jnp.float32
    ) + inner_shift.astype(jnp.float32)
    active_float, gelu_back = jax.vjp(gelu_tanh, inner)
    active = active_float.astype(jnp.bfloat16)
    outer_terms = jnp.dot(active, outer_used, preferred_element_type=jnp.float32)
    outer = outer_terms + outer_bias.astype(jnp.float32)
    result, second_back = jax.vjp(
        layer_norm,
        hidden + outer,
        second_gain.astype(jnp.float32),
        second_shift.astype(jnp.float32),
    )
    shaped = result.reshape(seq_count, -1, width)
    content_out = shaped[:, :split_at].astype(jnp.bfloat16)
    query_out = shaped[:, split_at:].astype(jnp.bfloat16)
    cotangent = (
        jnp.concatenate([content_cotangent, query_cotangent], axis=1)
        .astype(jnp.float32)
        .reshape(-1, width)
    )
    sum_grad, second_gain_grad, second_shift_grad = second_back(cotangent)
    outer_grad = sum_grad.astype(jnp.bfloat16)
    outer_bias_grad = jnp.sum(outer_grad.astype(jnp.float32), axis=0)
    outer_weight_part = jnp.dot(active.T, outer_grad, preferred_element_type=jnp.float32)
    active_grad = jnp.dot(outer_grad, outer_used.T, preferred_element_type=jnp.float32)
    inner_grad = gelu_back(active_grad)[0].astype(jnp.bfloat16)
    inner_bias_part = jnp.sum(inner_grad.astype(jnp.float32), axis=0)
    inner_weight_part = jnp.dot(hidden_low.T, inner_grad, preferred_element_type=jnp.float32)
    back_terms = jnp.dot(inner_grad, inner_used.T, preferred_element_type=jnp.float32)
    inner_weight_grad, inner_bias_grad, outer_weight_grad = (
        lax.psum_scatter(
            inner_weight_part.astype(jnp.bfloat16), "head", scatter_dimension=1, tiled=True
        ).astype(jnp.float32),
        lax.psum_scatter(
            inner_bias_part.astype(jnp.bfloat16), "head", scatter_dimension=0, tiled=True
        ).astype(jnp.float32),
        lax.psum_scatter(
            outer_weight_part.astype(jnp.bfloat16), "head", scatter_dimension=0, tiled=True
        ).astype(jnp.float32),
    )
    mixed_grad, first_gain_grad, first_shift_grad = first_back(sum_grad + back_terms)
    mixed_shaped = mixed_grad.reshape(seq_count, -1, width)
    attention_grad = mixed_shaped.astype(jnp.bfloat16)
    grad_content_rows, grad_query_rows = (
        lax.all_gather(attention_grad[:, :split_at], "head", axis=1, tiled=True),
        lax.all_gather(attention_grad[:, split_at:], "head", axis=1, tiled=True),
    )
    grad_stream = jnp.concatenate([grad_content_rows, grad_query_rows], axis=1)

    def attend_backward(carry, inputs):
        stream, joined, present, ranks, picks, labels, out_grad, log_total = inputs
        scores, visible, differ, offsets, query_word, query_place, query_label, keys, values = (
            score_block(stream, joined, present, ranks, picks, labels)
        )
        chances = jnp.exp(scores - log_total[:, :, None])
        soft_weights = chances.astype(jnp.bfloat16)
        attended = (
            jnp.einsum("hij,jhd->ihd", soft_weights, values, preferred_element_type=jnp.float32)
            .astype(jnp.bfloat16)
            .reshape(row_count, local_width)
        )
        output_part = jnp.dot(attended.T, out_grad, preferred_element_type=jnp.float32)
        attended_grad = (
            jnp.dot(out_grad, output_weight.T, preferred_element_type=jnp.float32)
            .astype(jnp.bfloat16)
            .reshape(row_count, heads, head_size)
        )
        chance_grad = jnp.einsum(
            "ihd,jhd->hij", attended_grad, values, preferred_element_type=jnp.float32
        )
        value_grad = (
            jnp.einsum(
                "hij,ihd->jhd", soft_weights, attended_grad, preferred_element_type=jnp.float32
            )
            .astype(jnp.bfloat16)
            .reshape(key_count, local_width)
        )
        score_grad = chances * (
            chance_grad - jnp.sum(chance_grad * chances, axis=-1, keepdims=True)
        )
        score_low = jnp.where(visible[None], score_grad, 0.0).astype(jnp.bfloat16) * score_scale
        word_grad = jnp.einsum("hij,jhd->ihd", score_low, keys, preferred_element_type=jnp.float32)
        key_grad = (
            jnp.einsum("hij,ihd->jhd", score_low, query_word, preferred_element_type=jnp.float32)
            .astype(jnp.bfloat16)
            .reshape(key_count, local_width)
        )
        place_scores = jnp.concatenate(
            [
                unshift_rows(score_low[:, :length], table_rows),
                unslide_rows(score_low[:, length:], offsets, table_rows),
            ],
            axis=1,
        )
        place_grad = jnp.einsum(
            "hir,rhd->ihd", place_scores, relative_keys, preferred_element_type=jnp.float32
        )
        relative_grad = (
            jnp.einsum(
                "hir,ihd->rhd", place_scores, query_place, preferred_element_type=jnp.float32
            )
            .astype(jnp.bfloat16)
            .reshape(table_rows, local_width)
        )
        score_float = score_low.astype(jnp.float32)
        other_sum = jnp.sum(jnp.where(differ[None], score_float, 0.0), axis=-1)
        same_sum = jnp.sum(jnp.where(differ[None], 0.0, score_float), axis=-1)
        label_grad = (
            same_sum.T[:, :, None] * segment_table[0][None]
            + other_sum.T[:, :, None] * segment_table[1][None]
        )
        embed_grad = jnp.stack(
            [
                jnp.einsum("hi,ihd->hd", same_sum, query_label, precision=highest),
                jnp.einsum("hi,ihd->hd", other_sum, query_label, precision=highest),
            ]
        )
        query_low = (
            (word_grad + place_grad + label_grad)
            .astype(jnp.bfloat16)
            .reshape(row_count, local_width)
        )
        row_grad = jnp.dot(query_low, query_weight.T, preferred_element_type=jnp.float32)
        joined_grad = jnp.dot(
            key_grad[memory_rows:], key_weight.T, preferred_element_type=jnp.float32
        ) + jnp.dot(value_grad[memory_rows:], value_weight.T, preferred_element_type=jnp.float32)
        row_grad = jnp.concatenate([row_grad[:length] + joined_grad, row_grad[length:]], axis=0)
        fresh = (
            jnp.dot(stream.T, query_low, preferred_element_type=jnp.float32),
            jnp.dot(joined.T, key_grad, preferred_element_type=jnp.float32),
            jnp.dot(joined.T, value_grad, preferred_element_type=jnp.float32),
            output_part,
            jnp.dot(position_table.T, relative_grad, preferred_element_type=jnp.float32),
            jnp.sum(word_grad, axis=0),
            jnp.sum(place_grad, axis=0),
            jnp.sum(label_grad, axis=0),
            embed_grad,
        )
        return (jax.tree.map(jnp.add, carry, fresh), row_grad)

    start_grads = (
        jnp.zeros(query_weight.shape, jnp.float32),
        jnp.zeros(key_weight.shape, jnp.float32),
        jnp.zeros(value_weight.shape, jnp.float32),
        jnp.zeros(output_weight.shape, jnp.float32),
        jnp.zeros(relative_weight.shape, jnp.float32),
        jnp.zeros(word_bias.shape, jnp.float32),
        jnp.zeros(position_bias.shape, jnp.float32),
        jnp.zeros(segment_bias.shape, jnp.float32),
        jnp.zeros(segment_embed.shape, jnp.float32),
    )
    attention_grads, row_grads = lax.scan(
        attend_backward,
        start_grads,
        (
            stream_rows,
            joined_rows,
            has_memory,
            order_rank,
            targets,
            segments,
            grad_stream,
            log_totals,
        ),
    )
    input_content, input_query = (
        lax.psum_scatter(
            row_grads[:, :length].astype(jnp.bfloat16), "head", scatter_dimension=1, tiled=True
        ).astype(jnp.float32),
        lax.psum_scatter(
            row_grads[:, length:].astype(jnp.bfloat16), "head", scatter_dimension=1, tiled=True
        ).astype(jnp.float32),
    )
    content_grad = mixed_shaped[:, :split_at] + input_content
    query_grad = mixed_shaped[:, split_at:] + input_query
    summed = lax.psum(
        (
            attention_grads[0],
            attention_grads[1],
            attention_grads[2],
            attention_grads[3],
            attention_grads[4],
            attention_grads[5],
            attention_grads[6],
            attention_grads[7],
            attention_grads[8],
            inner_weight_grad,
            inner_bias_grad,
            outer_weight_grad,
        ),
        "batch",
    )
    norms = lax.psum(
        (first_gain_grad, first_shift_grad, outer_bias_grad, second_gain_grad, second_shift_grad),
        ("head", "batch"),
    )
    return (
        content_out,
        query_out,
        content_grad,
        query_grad,
        summed[0],
        summed[1],
        summed[2],
        summed[3],
        summed[4],
        summed[5],
        summed[6],
        summed[7],
        summed[8],
        norms[0],
        norms[1],
        summed[9],
        summed[10],
        summed[11],
        norms[2],
        norms[3],
        norms[4],
    )


def solution(mesh):
    placed = (
        P("batch", "head", None),
        P("batch", "head", None),
        P("batch", "head", None),
        P("batch"),
        P("batch", None),
        P("batch", None),
        P("batch", None),
        P(None, "head"),
        P(None, "head"),
        P(None, "head"),
        P("head", None),
        P(None, "head"),
        P("head", None),
        P("head", None),
        P("head", None),
        P(None, "head", None),
        P(),
        P(),
        P(None, "head"),
        P("head"),
        P("head", None),
        P(),
        P(),
        P(),
        P("batch", "head", None),
        P("batch", "head", None),
    )
    return jax.shard_map(
        on_device,
        mesh=mesh,
        in_specs=placed,
        out_specs=(
            P("batch", "head", None),
            P("batch", "head", None),
            P("batch", "head", None),
            P("batch", "head", None),
            P(None, "head"),
            P(None, "head"),
            P(None, "head"),
            P("head", None),
            P(None, "head"),
            P("head", None),
            P("head", None),
            P("head", None),
            P(None, "head", None),
            P(),
            P(),
            P(None, "head"),
            P("head"),
            P("head", None),
            P(),
            P(),
            P(),
        ),
        check_vma=False,
    )
```

profile of v0, /device:TPU:0, one launch (start us, length us, event | category | flops | bytes accessed | tf_op | source)
XLA Modules:
  0.0 1517.7 jit_solution(834100053467898549)
XLA Ops:
  7.3 10.4 all_gather.25
  17.7 5.5 all_gather.26
  24.6 8.5 fusion.13
  36.9 3.9 slice.149
  40.8 52.3 %copy.60 = f32[3,96,1408]{0,1,2:T(8,128)} copy(f32[3,96,1408]{2,1,0:T(8,128)S(1)} %slice.152) | data formatting | bytes 3244032 | tf_op jit(solution)/shard_map/while/body/eval_jaxpr/slice | solution.py:163
  93.1 64.2 %gather_fusion = f32[96,3,896]{1,0,2:T(8,128)} fusion(f32[3,96,1408]{0,1,2:T(8,128)} %copy.60, s32[96]{0:T(128)S(1)} %get-tuple-element.294), kind=kCustom, calls=%fused_computation | custom fusion | bytes 2065152 | tf_op jit(solution)/shard_map/while/body/eval_jaxpr/vmap(vmap())/gather | solution.py:54
  157.3 30.2 %copy.61 = f32[96,3,896]{2,0,1:T(8,128)S(1)} copy(f32[96,3,896]{1,0,2:T(8,128)} %gather_fusion) | data formatting | bytes 2064384 | tf_op jit(solution)/shard_map/while/body/eval_jaxpr/vmap(vmap())/gather | solution.py:54
  187.5 9.9 reshape.377
  197.5 8.4 slice.150
  205.8 13.0 reshape.378
  220.4 7.6 all_gather.24
  231.4 2.8 fusion.83
  242.5 5.6 all-gather
  248.8 12.2 reduce-scatter.9.cloned.1.call-done
  261.0 31.5 %reduce-scatter.7.cloned.1.call-done = f32[1,128,768]{2,1,0:T(8,128)} async-done(((f32[1,512,768]{2,1,0:T(8,128)}), f32[1,128,768]{2,1,0:T(8,128)}) %reduce-scatter.7.cloned.1.call-update) | async-done | bytes 393232 | tf_op jit(solution)/shard_map/reduce_scatter | solution.py:204
  293.9 37.7 %all-gather.4.cloned.1.call-done = bf16[768,3072]{1,0:T(8,128)(2,1)} async-done(((bf16[768,768]{1,0:T(8,128)(2,1)}), bf16[768,3072]{1,0:T(8,128)(2,1)}) %all-gather.4.cloned.1.call-update) | async-done | bytes 4718608 | tf_op jit(solution)/shard_map/all_gather | solution.py:217
  331.6 3.3 convolution_add_fusion
  334.9 35.6 %all-gather.6.cloned.1.call-done = bf16[3072,768]{1,0:T(8,128)(2,1)} async-done(((bf16[768,768]{1,0:T(8,128)(2,1)}), bf16[3072,768]{1,0:T(8,128)(2,1)}) %all-gather.6.cloned.1.call-update) | async-done | bytes 4718608 | tf_op jit(solution)/shard_map/all_gather | solution.py:219
  370.5 3.9 fusion.84
  377.1 3.2 fusion.74
  384.0 8.6 all_gather.30
  392.7 5.6 all_gather.31
  398.8 13.3 fusion.1
  416.7 4.8 convolution_convert_fusion.6
  425.4 9.9 reshape.439
  435.3 7.0 reshape.383
  442.3 5.3 concatenate.103
  451.8 674.2 %while.1 = (s32[]{:T(128)}, bf16[3,96,1408]{2,0,1:T(4,128)(2,1)S(1)}, s32[96,2]{0,1:T(2,128)S(1)}, bf16[96,3,896]{2,1,0:T(4,128)(2,1)}, s32[]{:T(128)}, /*index=5*/s32[3]{0:T(128)S(1)}, s32[1]{0:T(128)}, s32[]{:T(128)}) while((s32[]{:T(128)}, bf16[3,96,1408]{2,0,1:T(4,128)(2,1)S(1)}, s32[96,2]{0,1:T(2,128)S(1)}, bf16[96,3,896]{2,1,0:T(4,128)(2,1)}, ...), condition=%wide.while_cond, body=%wide.while_body.sunk | while | flops 2707 | bytes 27043 | solution.py:62
  468.4 2.7 bitcast_select_fusion.2
  496.5 2.7 bitcast_select_fusion.2
  601.7 2.7 bitcast_select_fusion.2
  629.7 2.7 bitcast_select_fusion.2
  734.9 2.7 bitcast_select_fusion.2
  762.9 2.7 bitcast_select_fusion.2
  868.1 2.7 bitcast_select_fusion.2
  896.2 2.7 bitcast_select_fusion.2
  917.2 2.7 bitcast_select_fusion.2
  959.3 2.7 bitcast_select_fusion.2
  994.5 2.7 bitcast_select_fusion.2
  1128.0 4.8 fusion.81
  1136.6 5.5 convolution_convert_fusion
  1142.2 3.7 convolution_convert_fusion.1
  1146.8 4.2 convolution_convert_fusion.8
  1163.2 40.1 %all-reduce.5 = (f32[768]{0:T(1024)}, f32[768]{0:T(1024)}, f32[768]{0:T(1024)}, f32[768]{0:T(1024)}, f32[768]{0:T(1024)}) all-reduce(f32[768]{0:T(1024)S(1)} %copy-done.57, f32[768]{0:T(1024)S(1)} %copy-done.58, f32[768]{0:T(1024)S(1)} %copy-done.56, ...), channel_id=1, replica_groups=mesh['head'=4,'batch'=8] {'head','batch'}, use_global_device_ids=true, to_apply=%region_33.34 | all-reduce | flops 3840 | bytes 30720 | tf_op jit(solution)/shard_map/psum | solution.py:414
  1203.4 7.7 all-reduce.4
  1214.3 17.7 %reduce-scatter.17.cloned.1.call-done = bf16[768,768]{1,0:T(8,128)(2,1)} async-done(((bf16[3072,768]{1,0:T(8,128)(2,1)}), bf16[768,768]{1,0:T(8,128)(2,1)}) %reduce-scatter.17.cloned.1.call-update) | async-done | bytes 1179664 | tf_op jit(solution)/shard_map/reduce_scatter | solution.py:258
  1232.0 50.4 %reduce-scatter.15.cloned.1.call-done = bf16[768,768]{1,0:T(8,128)(2,1)} async-done(((bf16[768,3072]{1,0:T(8,128)(2,1)}), bf16[768,768]{1,0:T(8,128)(2,1)}) %reduce-scatter.15.cloned.1.call-update) | async-done | bytes 1179664 | tf_op jit(solution)/shard_map/reduce_scatter | solution.py:252
  1282.4 221.2 %all-reduce.12 = (f32[3,64]{1,0:T(4,128)}, f32[3,64]{1,0:T(4,128)}, f32[3,64]{1,0:T(4,128)}, f32[2,3,64]{2,1,0:T(4,128)S(1)}, f32[768,768]{1,0:T(8,128)}, /*index=5*/f32[768]{0:T(1024)}, f32[768,768]{1,0:T(8,128)}) all-reduce(f32[3,64]{1,0:T(4,128)S(1)} %copy-done.62, ...), channel_id=1, replica_groups=mesh['head'=4,'batch'=8] {'batch'}, use_global_device_ids=true, to_apply=%region_26.27 | all-reduce | flops 1181376 | bytes 7091712 | tf_op jit(solution)/shard_map/psum | solution.py:397
  (761 shorter events, 709.1 us)
Async XLA Ops:
  7.2 16.0 %copy-start = (bf16[768,192]{0,1:T(8,128)(2,1)S(1)}, bf16[768,192]{0,1:T(8,128)(2,1)}, u32[]{:S(2)}) copy-start(bf16[768,192]{0,1:T(8,128)(2,1)} %param.33) | copy-start | bytes 884740
  7.2 10.5 copy-start.47
  7.2 16.0 %copy-start.71 = (bf16[3,64]{1,0:T(4,128)(2,1)S(1)}, bf16[3,64]{1,0:T(4,128)(2,1)}, u32[]{:S(2)}) copy-start(bf16[3,64]{1,0:T(4,128)(2,1)} %param.40) | copy-start | bytes 1156
  7.2 16.5 %copy-start.52 = (bf16[2,3,64]{2,0,1:T(2,128)(2,1)S(1)}, bf16[2,3,64]{2,0,1:T(2,128)(2,1)}, u32[]{:S(2)}) copy-start(bf16[2,3,64]{2,0,1:T(2,128)(2,1)} %param.41) | copy-start | bytes 2308
  7.2 253.8 %reduce-scatter.9.cloned.1.call-start = ((), (), s32[]{:S(2)}) async-start(), calls=%async_computation.7 | async-start | bytes 368640 | tf_op jit(solution)/shard_map/reduce_scatter | solution.py:205
  17.7 211.0 %copy-start.5 = (bf16[1,512,768]{2,1,0:T(8,128)(2,1)}, bf16[1,512,768]{2,1,0:T(8,128)(2,1)S(1)}, u32[]{:S(2)}) copy-start(bf16[1,512,768]{2,1,0:T(8,128)(2,1)S(1)} %all_gather.25) | copy-start | bytes 2359300
  17.7 6.9 copy-start.72
  23.2 9.8 copy-start.48
  23.2 9.8 copy-start.3
  23.3 9.8 copy-start.76
  40.8 52.3 %copy-start.74 = (s32[1,96]{1,0:T(1,128)S(1)}, s32[1,96]{1,0:T(1,128)}, u32[]{:S(2)}) copy-start(s32[1,96]{1,0:T(1,128)} %param.31) | copy-start | bytes 1156
  218.8 9.2 copy-start.73
  218.8 9.2 copy-start.40
  218.8 9.8 copy-start.38
  229.3 6.5 copy-start.32
  229.7 4.5 copy-start.30
  239.7 52.8 %reduce-scatter.7.cloned.1.call-start = ((), (), s32[]{:S(2)}) async-start(), calls=%async_computation.6 | async-start | bytes 1966080 | tf_op jit(solution)/shard_map/reduce_scatter | solution.py:204
  241.0 7.1 copy-start.67
  241.0 7.1 copy-start.68
  241.0 7.1 copy-start.69
  241.0 51.5 %copy-start.24 = (bf16[1,128,768]{2,1,0:T(8,128)(2,1)S(1)}, bf16[1,128,768]{2,1,0:T(8,128)(2,1)}, u32[]{:S(2)}) copy-start(bf16[1,128,768]{2,1,0:T(8,128)(2,1)} %param.26) | copy-start | bytes 589828
  241.1 90.5 %all-gather.4.cloned.1.call-start = ((), (), s32[]{:S(2)}) async-start(), calls=%async_computation.8 | async-start | bytes 5898240 | tf_op jit(solution)/shard_map/all_gather | solution.py:217
  241.8 128.7 %all-gather.6.cloned.1.call-start = ((), (), s32[]{:S(2)}) async-start(), calls=%async_computation.9 | async-start | bytes 5898240 | tf_op jit(solution)/shard_map/all_gather | solution.py:219
  242.4 968.8 %reduce-scatter.13.cloned.1.call-start = ((), (), s32[]{:S(2)}) async-start(), calls=%async_computation.11 | async-start | bytes 184320 | tf_op jit(solution)/shard_map/reduce_scatter | solution.py:391
  334.9 39.5 %copy-start.10 = (f32[152,3072]{1,0:T(8,128)}, f32[152,3072]{1,0:T(8,128)S(1)}, u32[]{:S(2)}) copy-start(f32[152,3072]{1,0:T(8,128)S(1)} %convolution_add_fusion) | copy-start | bytes 5603332
  334.9 39.7 %copy-start.23 = (bf16[1,128,768]{2,1,0:T(8,128)(2,1)S(1)}, bf16[1,128,768]{2,1,0:T(8,128)(2,1)}, u32[]{:S(2)}) copy-start(bf16[1,128,768]{2,1,0:T(8,128)(2,1)} %param.50) | copy-start | bytes 589828
  334.9 39.7 %copy-start.43 = (bf16[1,24,768]{2,1,0:T(8,128)(2,1)S(1)}, bf16[1,24,768]{2,1,0:T(8,128)(2,1)}, u32[]{:S(2)}) copy-start(bf16[1,24,768]{2,1,0:T(8,128)(2,1)} %param.51) | copy-start | bytes 110596
  370.5 6.6 copy-start.75
  382.7 15.6 %copy-start.37 = (bf16[192,768]{1,0:T(8,128)(2,1)S(1)}, bf16[192,768]{1,0:T(8,128)(2,1)}, u32[]{:S(2)}) copy-start(bf16[192,768]{1,0:T(8,128)(2,1)} %param.36) | copy-start | bytes 884740
  392.7 19.4 %copy-start.21 = (bf16[1,512,768]{2,1,0:T(8,128)(2,1)}, bf16[1,512,768]{2,1,0:T(8,128)(2,1)S(1)}, u32[]{:S(2)}) copy-start(bf16[1,512,768]{2,1,0:T(8,128)(2,1)S(1)} %all_gather.30) | copy-start | bytes 2359300
  398.3 13.8 copy-start.44
  416.7 4.8 copy-start.61
  1135.5 77.1 %reduce-scatter.11.cloned.1.call-start = ((), (), s32[]{:S(2)}) async-start(), calls=%async_computation.10 | async-start | bytes 983040 | tf_op jit(solution)/shard_map/reduce_scatter | solution.py:388
  1136.6 95.4 %reduce-scatter.17.cloned.1.call-start = ((), (), s32[]{:S(2)}) async-start(), calls=%async_computation.13 | async-start | bytes 5898240 | tf_op jit(solution)/shard_map/reduce_scatter | solution.py:258
  1142.1 140.3 %reduce-scatter.15.cloned.1.call-start = ((), (), s32[]{:S(2)}) async-start(), calls=%async_computation.12 | async-start | bytes 5898240 | tf_op jit(solution)/shard_map/reduce_scatter | solution.py:252
  1145.9 5.2 copy-start.22
  1145.9 5.2 copy-start.45
  1145.9 6.4 copy-start.6
  1145.9 6.4 copy-start.20
  1145.9 358.3 %all-reduce.11.cloned.1.call-start = ((), (), s32[]{:S(2)}) async-start(), calls=%async_computation.14 | async-start | bytes 5898240 | tf_op jit(solution)/shard_map/psum | solution.py:397
  1146.8 5.5 copy-start.26
  1146.8 8.1 slice-start
  1159.2 44.1 %copy-start.64 = (bf16[3072]{0:T(1024)(128)(2,1)S(1)}, bf16[3072]{0:T(1024)(128)(2,1)}, u32[]{:S(2)}) copy-start(bf16[3072]{0:T(1024)(128)(2,1)} %get-tuple-element.286) | copy-start | bytes 18436
  1159.2 52.0 %copy-start.12 = (f32[1,152,768]{2,1,0:T(8,128)S(1)}, f32[1,152,768]{2,1,0:T(8,128)}, u32[]{:S(2)}) copy-start(f32[1,152,768]{2,1,0:T(8,128)} %get-tuple-element.303) | copy-start | bytes 1400836
  1159.3 123.2 %copy-start.62 = (f32[3,64]{1,0:T(4,128)S(1)}, f32[3,64]{1,0:T(4,128)}, u32[]{:S(2)}) copy-start(f32[3,64]{1,0:T(4,128)} %get-tuple-element.300) | copy-start | bytes 2308
  1159.3 123.2 %copy-start.63 = (f32[3,64]{1,0:T(4,128)S(1)}, f32[3,64]{1,0:T(4,128)}, u32[]{:S(2)}) copy-start(f32[3,64]{1,0:T(4,128)} %get-tuple-element.304) | copy-start | bytes 2308
  1504.3 4.8 copy-start.28
  1504.3 5.6 copy-start.27
  (44 other events, 102.2 us)
Sparse Core Ops, SparseCore 0:
  239.8 21.1 reduce-scatter.8
  264.3 28.1 reduce-scatter.6
  294.1 37.4 all-gather.3
  333.0 37.4 all-gather.5
  1135.6 19.7 reduce-scatter.12
  1157.8 23.4 reduce-scatter.10
  1184.0 48.0 reduce-scatter.16
  1234.6 47.8 reduce-scatter.14
  1288.3 206.9 all-reduce.10
where the time goes:
time: 1530 us; the launch traced here: 1520 us
  other arithmetic  473 us (31%)
  local copies, waits for them, and re-layouts  454 us (30%)
  blocking collectives  312 us (20%)
  waiting for transfers between devices  186 us (12%)
  matrix products  72.4 us (5%)
  between operations  16.7 us (1%)
    scatter x192, other arithmetic  453 us
    psum x1, blocking collectives, on_device(): lax.psum((attention_grads[0], attention_grads[1], attention_grads[2], att...  221 us
    scatter x288, local copies, waits for them, and re-layouts  219 us
    gather x2, local copies, waits for them, and re-layouts, slide_one_row(): return lax.dynamic_slice_in_dim(row, start, width)  94.5 us
    slice x2, local copies, waits for them, and re-layouts, score_block(): relative_all[:, length:]  52.4 us
    reduce_scatter x1, waiting for transfers between devices, on_device(): lax.psum_scatter(inner_weight_part.astype(jnp.bfloat16), 'head', scatter_...  50.4 us
    psum x1, blocking collectives, on_device(): lax.psum((first_gain_grad, first_shift_grad, outer_bias_grad, second_gain...  40.1 us
    all_gather x1, waiting for transfers between devices, on_device(): lax.all_gather(inner_weight, 'head', axis=1, tiled=True)  37.7 us
  transfers between devices with their start and end apart: 9, of which 6 were waited for; matrix products, arithmetic and copies ran while one was open for 2% of the time, Pallas kernels for 0%

commit v1 on v0

v1 whole, which is shorter than its diff:
```python
import functools
import jax
import jax.numpy as jnp
import numpy as np
from jax import lax
from jax.experimental import pallas as pl
from jax.experimental.pallas import tpu as pltpu
from jax.sharding import PartitionSpec as P

masked_score = -1e30
norm_eps = 1e-05
gelu_root = 0.7978845608028654
gelu_cubic = 0.044715
hidden_key = 1 << 20
F32 = jnp.float32
BF16 = jnp.bfloat16
MIB = 1024 * 1024


def dot_nt(a, b):
    return lax.dot_general(a, b, (((1,), (1,)), ((), ())), preferred_element_type=F32)


def dot_nn(a, b):
    return lax.dot_general(a, b, (((1,), (0,)), ((), ())), preferred_element_type=F32)


def dot_tn(a, b):
    return lax.dot_general(a, b, (((0,), (0,)), ((), ())), preferred_element_type=F32)


def position_rows(key_count, length, width):
    steps = key_count - 1 - np.arange(key_count + length, dtype=np.float64)
    freqs = 10000.0 ** (-np.arange(0, width, 2, dtype=np.float64) / width)
    angles = steps[:, None] * freqs[None, :]
    return np.concatenate([np.sin(angles), np.cos(angles)], axis=1).astype(jnp.bfloat16)


def whole(shape):
    return pl.BlockSpec(shape, lambda *_: (0,) * len(shape))


def call(kernel, name, grid, ins, in_specs, outs, out_specs, scratch=()):
    return pl.pallas_call(
        kernel,
        grid=grid,
        in_specs=in_specs,
        out_specs=out_specs,
        out_shape=[jax.ShapeDtypeStruct(s, t) for s, t in outs],
        scratch_shapes=list(scratch),
        compiler_params=pltpu.CompilerParams(vmem_limit_bytes=52 * MIB),
        name=name,
    )(*ins)


def attend_forward_kernel(
    blocks, head_size, length,
    stream_ref, joined_ref, wq_ref, wkv_ref, rel_ref, col_ref, row_ref, bias_ref, embed_ref, keycol_ref,
    p_ref, att_ref, qf_ref, kc_ref, v_ref, acc_ref,
):
    h = pl.program_id(0)
    keys = joined_ref.shape[0]
    wide = wq_ref.shape[1]

    @pl.when(h == 0)
    def _():
        qf_ref[...] = dot_nn(stream_ref[...], wq_ref[...])
        kv = dot_nn(joined_ref[...], wkv_ref[...])
        kc_ref[...] = (kv[:, :wide] + keycol_ref[...].astype(F32)).astype(BF16)
        v_ref[...] = kv[:, wide:].astype(BF16)
        acc_ref[...] = jnp.zeros_like(acc_ref)

    limit_row = row_ref[0:1, :]
    for start, size, position in blocks:
        blk = slice(start, start + size)
        lane = lax.broadcasted_iota(jnp.int32, (size, wide), 1)
        mine = (lane >= h * head_size) & (lane < (h + 1) * head_size)
        qf = qf_ref[blk, :]
        zero = jnp.zeros_like(qf)
        word = jnp.where(mine, (qf + bias_ref[0:1, :]).astype(BF16).astype(F32) * 0.125, zero)
        place = jnp.where(mine, qf + bias_ref[1:2, :], zero).astype(BF16) * 0.125
        label = jnp.where(mine, (qf + bias_ref[2:3, :]) * 0.125, zero)
        label_hi = label.astype(BF16)
        label_lo = (label - label_hi.astype(F32)).astype(BF16)
        both = dot_nn(label_hi, embed_ref[...]) + dot_nn(label_lo, embed_ref[...])
        row_label = col_ref[blk, 1:2]
        pair = jnp.where(row_label == 0, both[:, :wide], both[:, wide:])
        pair_hi = pair.astype(BF16).astype(F32)
        first = wide - head_size
        hi_lane = (lane == first) | (lane == first + 2)
        lo_lane = (lane == first + 1) | (lane == first + 3)
        query = jnp.where(hi_lane, pair_hi, jnp.where(lo_lane, pair - pair_hi, word)).astype(BF16)
        scores = dot_nt(query, kc_ref[...])
        if position is not None:
            base = length - position - size
            width = keys + size
            rel = dot_nt(place, rel_ref[base : base + width, :])
            rel = pltpu.roll(rel, width - (size - 1), 1, stride=1, stride_axis=0)
        else:
            rel = dot_nt(place, rel_ref[...])
            total = rel.shape[1]
            shift = col_ref[blk, 2:3]
            bit = 0
            while (1 << bit) < length:
                rel = jnp.where(((shift >> bit) & 1) == 1, pltpu.roll(rel, total - (1 << bit), 1), rel)
                bit += 1
        scores = scores + rel[:, :keys]
        limit = col_ref[blk, 0:1]
        scores = jnp.where(limit_row < limit, scores, masked_score)
        top = jnp.max(scores, axis=-1, keepdims=True)
        powers = jnp.exp(scores - top)
        total = jnp.sum(powers, axis=-1, keepdims=True)
        soft = (powers * (1.0 / total)).astype(BF16)
        p_ref[0, blk, :] = soft
        att = dot_nn(soft, v_ref[...])
        acc_ref[blk, :] = jnp.where(mine, att, acc_ref[blk, :])

    @pl.when(h == pl.num_programs(0) - 1)
    def _():
        att_ref[...] = acc_ref[:, : att_ref.shape[1]].astype(BF16)


def attend_forward(blocks, stream, joined, wq, wkv, rel, col, row, bias, embed, keycol, heads, head_size, length):
    rows, keys, wide = stream.shape[0], joined.shape[0], wq.shape[1]
    ins = (stream, joined, wq, wkv, rel, col, row, bias, embed, keycol)
    outs = [
        ((heads, rows, keys), BF16),
        ((rows, heads * head_size), BF16),
        ((rows, wide), F32),
        ((keys, wide), BF16),
        ((keys, wide), BF16),
    ]
    out_specs = [pl.BlockSpec((1, rows, keys), lambda h: (h, 0, 0))] + [whole(s) for s, _ in outs[1:]]
    return call(
        functools.partial(attend_forward_kernel, blocks, head_size, length),
        "attend_forward", (heads,), ins, [whole(x.shape) for x in ins], outs, out_specs,
        [pltpu.VMEM((rows, wide), F32)],
    )


def attend_backward_kernel(
    blocks, head_size, length,
    p_ref, dat_ref, da_ref, qf_ref, qft_ref, kc_ref, v_ref, rel_ref, col_ref, bias_ref, biast_ref, embed_ref,
    dq_ref, kg_ref, vg_ref, rg_ref, small_ref, word_acc, place_acc, label_acc, s_scr, rg_acc,
):
    h = pl.program_id(0)
    keys = kc_ref.shape[0]
    wide = kc_ref.shape[1]
    total_rel = rel_ref.shape[0]
    heads = pl.num_programs(0)
    local = da_ref.shape[1]

    @pl.when(h == 0)
    def _():
        word_acc[...] = jnp.zeros_like(word_acc)
        place_acc[...] = jnp.zeros_like(place_acc)
        label_acc[...] = jnp.zeros_like(label_acc)
        small_ref[...] = jnp.zeros_like(small_ref)

    qft = qft_ref[...]
    word_t = (qft + biast_ref[:, 0:1]).astype(BF16) * 0.125
    place_t = (qft + biast_ref[:, 1:2]).astype(BF16) * 0.125
    rg_acc[...] = jnp.zeros_like(rg_acc)
    first = wide - head_size
    vg_ref[...] = dot_nn(dat_ref[...], p_ref[0]).astype(BF16)
    for start, size, position in blocks:
        blk = slice(start, start + size)
        lane = lax.broadcasted_iota(jnp.int32, (size, wide), 1)
        mine = (lane >= h * head_size) & (lane < (h + 1) * head_size)
        soft = p_ref[0, blk, :].astype(F32)
        grad = jnp.where(mine[:, :local], da_ref[blk, :], 0)
        chance = dot_nt(grad, v_ref[:, :local])
        inner = jnp.sum(chance * soft, axis=-1, keepdims=True)
        score = (soft * (chance - inner)).astype(BF16)
        s_scr[blk, :] = score
        word = dot_nn(score, kc_ref[...]) * 0.125
        word_acc[blk, :] = jnp.where(mine, word, word_acc[blk, :])
        if position is not None:
            base = length - position - size
            width = keys + size
            left = (size - 1) - lax.broadcasted_iota(jnp.int32, (size, 1), 0)
            reach = size
        else:
            base = 0
            width = total_rel
            left = col_ref[blk, 2:3]
            reach = length
        wider = jnp.concatenate([score.astype(F32), jnp.zeros((size, width - keys), F32)], axis=1)
        bit = 0
        while (1 << bit) < reach:
            wider = jnp.where(((left >> bit) & 1) == 1, pltpu.roll(wider, 1 << bit, 1), wider)
            bit += 1
        wider = wider.astype(BF16)
        placed = dot_nn(wider, rel_ref[base : base + width, :]) * 0.125
        place_acc[blk, :] = jnp.where(mine, placed, place_acc[blk, :])
        rg_acc[:, base : base + width] += dot_nn(place_t[:, blk], wider)
        zero_key = word[:, first : first + 1]
        one_key = word[:, first + 2 : first + 3]
        row_label = col_ref[blk, 1:2]
        same = jnp.where(row_label == 0, zero_key, one_key)
        other = jnp.where(row_label == 0, one_key, zero_key)
        label = same * embed_ref[0:1, :] + other * embed_ref[1:2, :]
        label_acc[blk, :] = jnp.where(mine, label, label_acc[blk, :])
        query_label = qf_ref[blk, :] + bias_ref[2:3, :]
        on = mine[0:1, :]
        small_ref[3:4, :] += jnp.where(on, jnp.sum(query_label * same, axis=0, keepdims=True), 0.0)
        small_ref[4:5, :] += jnp.where(on, jnp.sum(query_label * other, axis=0, keepdims=True), 0.0)
    kg_ref[...] = dot_nn(word_t, s_scr[...]).astype(BF16)
    rg_ref[...] = rg_acc[...].astype(BF16)

    @pl.when(h == heads - 1)
    def _():
        word, place, label = word_acc[...], place_acc[...], label_acc[...]
        dq_ref[...] = (word + place + label)[:, :local].astype(BF16)
        small_ref[0:1, :] = jnp.sum(word, axis=0, keepdims=True)
        small_ref[1:2, :] = jnp.sum(place, axis=0, keepdims=True)
        small_ref[2:3, :] = jnp.sum(label, axis=0, keepdims=True)


def attend_backward(blocks, p, dat, da, qf, qft, kc, v, rel, col, bias, biast, embed, head_size, length):
    heads, rows, keys = p.shape
    wide = qf.shape[1]
    local = heads * head_size
    total_rel = rel.shape[0]
    ins = (p, dat, da, qf, qft, kc, v, rel, col, bias, biast, embed)
    specs = [whole(x.shape) for x in ins]
    specs[0] = pl.BlockSpec((1, rows, keys), lambda h: (h, 0, 0))
    specs[1] = pl.BlockSpec((head_size, rows), lambda h: (h, 0))
    specs[4] = pl.BlockSpec((head_size, rows), lambda h: (h, 0))
    specs[10] = pl.BlockSpec((head_size, biast.shape[1]), lambda h: (h, 0))
    outs = [
        ((rows, local), BF16),
        ((local, keys), BF16),
        ((local, keys), BF16),
        ((local, total_rel), BF16),
        ((8, wide), F32),
    ]
    out_specs = [whole((rows, local))]
    out_specs += [pl.BlockSpec((head_size, n), lambda h: (h, 0)) for n in (keys, keys, total_rel)]
    out_specs += [whole((8, wide))]
    return call(
        functools.partial(attend_backward_kernel, blocks, head_size, length),
        "attend_backward", (heads,), ins, specs, outs, out_specs,
        [pltpu.VMEM((rows, wide), F32)] * 3
        + [pltpu.VMEM((rows, keys), BF16), pltpu.VMEM((head_size, total_rel), F32)],
    )


def norm_parts(x):
    center = x - jnp.mean(x, axis=-1, keepdims=True)
    scale = lax.rsqrt(jnp.mean(center * center, axis=-1, keepdims=True) + norm_eps)
    return center * scale, scale


def norm_back(grad, gain, unit, scale):
    along = grad * gain
    return scale * (
        along
        - jnp.mean(along, axis=-1, keepdims=True)
        - unit * jnp.mean(along * unit, axis=-1, keepdims=True)
    )


def feed_forward_kernel(
    core_ref, a0_ref, a1_ref, a2_ref, a3_ref, w0_ref, w1_ref, w2_ref, w3_ref, stream_ref, vec_ref,
    wi_ref, bi_ref, wo_ref,
    hid_ref, act_ref, gp_ref, mixed_ref, mine_ref, other_ref,
):
    half = mine_ref.shape[0]
    core = core_ref[0]
    for step in range(2):
        rows = pl.ds(pl.multiple_of((core if step else 1 - core) * half, 16), half)
        out = dot_nn(a0_ref[rows, :], w0_ref[...]) + dot_nn(a1_ref[rows, :], w1_ref[...])
        out = out + dot_nn(a2_ref[rows, :], w2_ref[...]) + dot_nn(a3_ref[rows, :], w3_ref[...])
        mixed = stream_ref[rows, :].astype(F32) + out
        if step:
            mixed_ref[...] = mixed
        unit, _ = norm_parts(mixed)
        hidden = (unit * vec_ref[0:1, :] + vec_ref[1:2, :]).astype(BF16)
        hid_ref[rows, :] = hidden
        inner = dot_nn(hidden, wi_ref[...]) + bi_ref[0:1, :]
        square = inner * inner
        turn = jnp.tanh(gelu_root * (inner + gelu_cubic * square * inner))
        lift = 0.5 * (1.0 + turn)
        slope = lift + 0.5 * inner * (1.0 - turn * turn) * (gelu_root * (1.0 + 3.0 * gelu_cubic * square))
        active = (inner * lift).astype(BF16)
        act_ref[rows, :] = active
        gp_ref[rows, :] = slope.astype(BF16)
        part = dot_nn(active, wo_ref[...]).astype(BF16)
        if step:
            mine_ref[...] = part
        else:
            other_ref[...] = part


def feed_forward(core, atts, wos, stream, vec, wi, bi, wo):
    rows, width = stream.shape
    units = wi.shape[1]
    half = rows // 2
    ins = (core, *atts, *wos, stream, vec, wi, bi, wo)
    outs = [
        ((rows, width), BF16),
        ((rows, units), BF16),
        ((rows, units), BF16),
        ((half, width), F32),
        ((half, width), BF16),
        ((half, width), BF16),
    ]
    specs = [pl.BlockSpec(memory_space=pltpu.SMEM)] + [whole(x.shape) for x in ins[1:]]
    return call(feed_forward_kernel, "feed_forward", (1,), ins, specs, outs, [whole(s) for s, _ in outs])


def second_norm_kernel(a_ref, b_ref, mixed_ref, cot_ref, vec_ref, out_ref, og_ref, sg_ref, sums_ref):
    unit, _ = norm_parts(mixed_ref[...])
    hidden = unit * vec_ref[0:1, :] + vec_ref[1:2, :]
    total = a_ref[...].astype(F32) + b_ref[...].astype(F32)
    unit, scale = norm_parts(hidden + total + vec_ref[2:3, :])
    out_ref[...] = (unit * vec_ref[3:4, :] + vec_ref[4:5, :]).astype(BF16)
    cot = cot_ref[...].astype(F32)
    grad = norm_back(cot, vec_ref[3:4, :], unit, scale)
    low = grad.astype(BF16)
    og_ref[...] = low
    sg_ref[...] = grad
    sums_ref[...] = jnp.zeros_like(sums_ref)
    sums_ref[0:1, :] = jnp.sum(low.astype(F32), axis=0, keepdims=True)
    sums_ref[1:2, :] = jnp.sum(cot * unit, axis=0, keepdims=True)
    sums_ref[2:3, :] = jnp.sum(cot, axis=0, keepdims=True)


def second_norm(a, b, mixed, cot, vec):
    ins = (a, b, mixed, cot, vec)
    shape = a.shape
    outs = [(shape, BF16), (shape, BF16), (shape, F32), ((8, shape[1]), F32)]
    return call(
        second_norm_kernel, "second_norm", (1,), ins, [whole(x.shape) for x in ins], outs,
        [whole(s) for s, _ in outs],
    )


def feed_backward_kernel(
    core_ref, mine_ref, other_ref, gp_ref, wi_ref, wo_ref, ig_ref, og_ref, bm_ref, bo_ref, sums_ref
):
    half = mine_ref.shape[0]
    core = core_ref[0]
    sums_ref[...] = jnp.zeros_like(sums_ref)
    for step in range(2):
        rows = pl.ds(pl.multiple_of((core if step else 1 - core) * half, 16), half)
        og = mine_ref[...] if step else other_ref[...]
        og_ref[rows, :] = og
        grad = (dot_nt(og, wo_ref[...]) * gp_ref[rows, :].astype(F32)).astype(BF16)
        ig_ref[rows, :] = grad
        sums_ref[0:1, :] += jnp.sum(grad.astype(F32), axis=0, keepdims=True)
        part = dot_nt(grad, wi_ref[...]).astype(BF16)
        if step:
            bm_ref[...] = part
        else:
            bo_ref[...] = part


def feed_backward(core, mine, other, gp, wi, wo):
    rows, units = gp.shape
    half, width = mine.shape
    ins = (core, mine, other, gp, wi, wo)
    outs = [
        ((rows, units), BF16),
        ((rows, width), BF16),
        ((half, width), BF16),
        ((half, width), BF16),
        ((8, units), F32),
    ]
    specs = [pl.BlockSpec(memory_space=pltpu.SMEM)] + [whole(x.shape) for x in ins[1:]]
    return call(feed_backward_kernel, "feed_backward", (1,), ins, specs, outs, [whole(s) for s, _ in outs])


def first_norm_kernel(a_ref, b_ref, sg_ref, mixed_ref, vec_ref, mg_ref, ag_ref, sums_ref):
    grad = sg_ref[...] + a_ref[...].astype(F32) + b_ref[...].astype(F32)
    unit, scale = norm_parts(mixed_ref[...])
    out = norm_back(grad, vec_ref[0:1, :], unit, scale)
    mg_ref[...] = out
    ag_ref[...] = out.astype(BF16)
    sums_ref[...] = jnp.zeros_like(sums_ref)
    sums_ref[0:1, :] = jnp.sum(grad * unit, axis=0, keepdims=True)
    sums_ref[1:2, :] = jnp.sum(grad, axis=0, keepdims=True)


def first_norm(a, b, sg, mixed, vec):
    ins = (a, b, sg, mixed, vec)
    shape = a.shape
    outs = [(shape, F32), (shape, BF16), ((8, shape[1]), F32)]
    return call(
        first_norm_kernel, "first_norm", (1,), ins, [whole(x.shape) for x in ins], outs,
        [whole(s) for s, _ in outs],
    )


def add_kernel(a_ref, b_ref, o_ref):
    o_ref[...] = (a_ref[...].astype(F32) + b_ref[...].astype(F32)).astype(BF16)


def on_device(
    content, query_stream, memory, has_memory, order_rank, targets, segments,
    query_weight, key_weight, value_weight, output_weight, relative_weight,
    word_bias, position_bias, segment_bias, segment_embed, first_gain, first_shift,
    inner_weight, inner_bias, outer_weight, outer_bias, second_gain, second_shift,
    content_cotangent, query_cotangent,
):
    parts = lax.axis_size("head")
    me = lax.axis_index("head")
    core = me % 2
    core_perm = [(i, i ^ 1) for i in range(parts)]
    x_perm = [(i, i ^ 2) for i in range(parts)]

    def swap_core(x):
        return lax.ppermute(x, "head", core_perm)

    def swap_x(x):
        return lax.ppermute(x, "head", x_perm)

    own, width = content.shape[1:]
    own_picks, own_memory = query_stream.shape[1], memory.shape[1]
    length, picks_n, mem = own * parts, own_picks * parts, own_memory * parts
    keys = mem + length
    heads, head_size = word_bias.shape
    local = heads * head_size
    wide = local + head_size
    half = 2 * (own + own_picks)
    rows = 2 * half

    gathered = lax.all_gather(
        jnp.concatenate([content[0], query_stream[0], memory[0]], axis=0), "head", axis=0, tiled=False
    )
    con, pik, mems = (
        gathered[:, :own],
        gathered[:, own : own + own_picks],
        gathered[:, own + own_picks :],
    )
    order = (0, 2, 1, 3)

    def lay(a, b):
        return jnp.concatenate([a[0], a[2], b[0], b[2], a[1], a[3], b[1], b[3]], axis=0)

    stream = lay(con, pik)
    joined = jnp.concatenate([mems.reshape(mem, width), con.reshape(length, width)], axis=0)
    blocks = (
        (0, own, 0),
        (own, own, 2 * own),
        (2 * own, 2 * own_picks, None),
        (half, own, own),
        (half + own, own, 3 * own),
        (half + 2 * own, 2 * own_picks, None),
    )

    ranks, picks, labels = order_rank[0], targets[0], segments[0]
    picked = picks[:, None] == jnp.arange(length, dtype=jnp.int32)[None, :]
    pick_rank = jnp.sum(jnp.where(picked, ranks[None, :], 0), axis=1)
    pick_label = jnp.sum(jnp.where(picked, labels[None, :], 0), axis=1)

    def lay_column(a, b):
        return lay(a.reshape(parts, own), b.reshape(parts, own_picks))

    limit = lay_column(ranks + 1, pick_rank)
    row_label = lay_column(labels, pick_label)
    shift = lay_column(jnp.zeros_like(ranks), length - 1 - picks)
    col = jnp.stack([limit, row_label, shift] + [shift] * 5, axis=1)
    memory_rank = jnp.where(has_memory[0] > 0, -1, hidden_key).astype(jnp.int32)
    row = jnp.broadcast_to(jnp.concatenate([jnp.full((mem,), memory_rank), ranks])[None], (8, keys))
    key_label = jnp.concatenate([jnp.zeros((mem,), jnp.int32), labels])
    lane = jnp.arange(wide)[None]
    zero_lane = (lane == local) | (lane == local + 1)
    one_lane = (lane == local + 2) | (lane == local + 3)
    keycol = jnp.where(
        zero_lane, (1 - key_label)[:, None], jnp.where(one_lane, key_label[:, None], 0)
    ).astype(BF16)
    bias = jnp.pad(
        jnp.stack([word_bias.reshape(-1), position_bias.reshape(-1), segment_bias.reshape(-1)]).astype(F32),
        ((0, 5), (0, wide - local)),
    )
    flat_embed = jnp.pad(segment_embed.reshape(2, local), ((0, 0), (0, wide - local)))

    def embed_lanes(a, b):
        return jnp.where(zero_lane, a[:, None], jnp.where(one_lane, b[:, None], 0))

    embed = jnp.concatenate(
        [embed_lanes(flat_embed[0], flat_embed[1]), embed_lanes(flat_embed[1], flat_embed[0])], axis=1
    ).astype(BF16)

    def widen(w):
        return jnp.pad(w, ((0, 0), (0, wide - local)))

    table = jnp.asarray(position_rows(keys, length, width))
    rel = jnp.dot(table, widen(relative_weight), preferred_element_type=F32).astype(BF16)
    wkv = jnp.concatenate([widen(key_weight), widen(value_weight)], axis=1)

    wo_core = swap_core(output_weight)
    wo_x = swap_x(output_weight)
    wo_diag = swap_core(wo_x)
    cot_own = jnp.concatenate([content_cotangent[0], query_cotangent[0]], axis=0)
    cot_x = swap_x(cot_own)
    first_x = me < 2
    cot_0 = jnp.where(first_x, cot_own, cot_x)
    cot_1 = jnp.where(first_x, cot_x, cot_own)
    cot = jnp.concatenate([cot_0[:own], cot_1[:own], cot_0[own:], cot_1[own:]], axis=0)

    p, att, qf, kc, v = attend_forward(
        blocks, stream, joined, widen(query_weight), wkv, rel, col, row, bias, embed, keycol,
        heads, head_size, length,
    )
    att_core = swap_core(att)
    att_x = swap_x(att)
    att_diag = swap_core(att_x)

    vec = jnp.stack(
        [first_gain, first_shift, outer_bias, second_gain, second_shift] + [second_shift] * 3
    ).astype(F32)
    bi = jnp.broadcast_to(inner_bias.astype(F32)[None], (8, inner_bias.shape[0]))
    core_id = core.astype(jnp.int32).reshape(1)
    hid, act, gp, mixed, part_mine, part_other = feed_forward(
        core_id, (att, att_core, att_x, att_diag), (output_weight, wo_core, wo_x, wo_diag), stream, vec,
        inner_weight, bi, outer_weight,
    )

    def add(a, b):
        return call(add_kernel, "add", (1,), (a, b), [whole(a.shape)] * 2, [(a.shape, BF16)], [whole(a.shape)])[0]

    chip_part = add(part_mine, swap_core(part_other))
    out_half, og_half, sg_half, sums2 = second_norm(chip_part, swap_x(chip_part), mixed, cot, vec)
    ig, og, back_mine, back_other, inner_sums = feed_backward(
        core_id, og_half, swap_core(og_half), gp, inner_weight, outer_weight
    )
    chip_back = add(back_mine, swap_core(back_other))
    outer_weight_part = dot_tn(act, og).astype(BF16)
    inner_weight_part = dot_tn(hid, ig).astype(BF16)
    mg_half, ag_half, sums1 = first_norm(chip_back, swap_x(chip_back), sg_half, mixed, vec)
    ag_other = swap_core(ag_half)
    ag = jnp.where(
        core == 0,
        jnp.concatenate([ag_half, ag_other], axis=0),
        jnp.concatenate([ag_other, ag_half], axis=0),
    )
    da = dot_nt(ag, output_weight).astype(BF16)
    dat = dot_nt(output_weight, ag).astype(BF16)
    dq, kg, vg, rg, small = attend_backward(
        blocks, p, dat, da, qf, qf[:, :local].T, kc, v, rel, col, bias, bias[:, :local].T,
        flat_embed.astype(F32), head_size, length,
    )

    row_part = dot_nt(dq, query_weight)
    key_part = dot_tn(
        jnp.concatenate([kg[:, mem:], vg[:, mem:]], axis=0),
        jnp.concatenate([key_weight, value_weight], axis=1).T,
    )
    zeros = jnp.zeros((parts, own_picks, width), F32)
    row_part = row_part + lay(key_part.reshape(parts, own, width), zeros)
    low_rows = row_part.astype(BF16)
    row_mine = jnp.where(core == 0, low_rows[:half], low_rows[half:])
    row_other = jnp.where(core == 0, low_rows[half:], low_rows[:half])
    chip_row = add(row_mine, swap_core(row_other))

    def pick(a, which):
        first_half = jnp.concatenate([a[:own], a[2 * own : 2 * own + own_picks]], axis=0)
        second_half = jnp.concatenate([a[own : 2 * own], a[2 * own + own_picks :]], axis=0)
        return jnp.where(which == 0, first_half, second_half)

    side = me // 2
    row_sum = pick(chip_row, side).astype(F32) + swap_x(pick(chip_row, 1 - side)).astype(F32)
    row_grad = pick(mg_half, side) + row_sum
    outs = pick(out_half, side)

    query_weight_part = dot_tn(stream, dq).astype(BF16)
    key_weight_part = dot_nn(kg, joined).astype(BF16)
    value_weight_part = dot_nn(vg, joined).astype(BF16)
    relative_weight_part = dot_nn(rg, table).astype(BF16)
    output_weight_part = dot_tn(att, ag).astype(BF16)
    norm_sums = sums2[:3], sums1[:2]
    norm_sums = jnp.concatenate(norm_sums, axis=0)
    norm_sums = norm_sums + swap_core(norm_sums)
    ff = lax.psum((outer_weight_part, inner_weight_part, inner_sums[0]), "batch")
    rest = lax.psum(
        (
            query_weight_part,
            key_weight_part,
            value_weight_part,
            relative_weight_part,
            output_weight_part,
            small[:5, :local],
            norm_sums,
        ),
        "batch",
    )
    small_sum, norm_sum = rest[5], rest[6]

    def per_head(a):
        return a.reshape(heads, head_size)

    return (
        outs[None, :own],
        outs[None, own:],
        row_grad[None, :own],
        row_grad[None, own:],
        rest[0].astype(F32),
        rest[1].astype(F32).T,
        rest[2].astype(F32).T,
        rest[4].astype(F32),
        rest[3].astype(F32).T,
        per_head(small_sum[0]),
        per_head(small_sum[1]),
        per_head(small_sum[2]),
        small_sum[3:5].reshape(2, heads, head_size),
        norm_sum[3],
        norm_sum[4],
        ff[1].astype(F32),
        ff[2],
        ff[0].astype(F32),
        norm_sum[0],
        norm_sum[1],
        norm_sum[2],
    )


def solution(mesh):
    rows = P("batch", "head", None)
    ids = P("batch", None)
    columns = P(None, "head")
    by_head = P("head", None)
    table = P(None, "head", None)
    return jax.shard_map(
        on_device,
        mesh=mesh,
        in_specs=(
            rows, rows, rows, P("batch"), ids, ids, ids,
            columns, columns, columns, by_head, columns,
            by_head, by_head, by_head, table, P(), P(),
            columns, P("head"), by_head, P(), P(), P(), rows, rows,
        ),
        out_specs=(
            rows, rows, rows, rows,
            columns, columns, columns, by_head, columns,
            by_head, by_head, by_head, table, P(), P(),
            columns, P("head"), by_head, P(), P(), P(),
        ),
        check_vma=False,
    )
```

time: 1530 us -> 330 us (0.22)
  other arithmetic: 473 us -> 19.4 us
  local copies, waits for them, and re-layouts: 454 us -> 20.1 us
  blocking collectives: 312 us -> 41.2 us
  Pallas kernels: 0 us -> 66.3 us
  matrix products: 72.4 us -> 16.5 us
  waiting for transfers between devices: 186 us -> 143 us
    scatter x193 -> x0, other arithmetic: 453 us -> none
    psum x2 -> x1, blocking collectives: 261 us -> 41.2 us  [on_device(): lax.psum((query_weight_part, key_weight_part, value_weight_part, relative...]
    scatter x288 -> x0, local copies, waits for them, and re-layouts: 219 us -> none
    reduce_scatter x6 -> x0, waiting for transfers between devices: 112 us -> none  [the longest x1 50.4 us: on_device(): lax.psum_scatter(inner_weight_part.astype(jnp.bfloat16), 'head', scatter_...]
    psum x1, waiting for transfers between devices: 0.01 us -> 99.3 us  [on_device(): lax.psum((query_weight_part, key_weight_part, value_weight_part, relative...]
    gather x2 -> x0, local copies, waits for them, and re-layouts: 94.5 us -> none  [slide_one_row(): return lax.dynamic_slice_in_dim(row, start, width)]
    slice x20 -> x25, local copies, waits for them, and re-layouts: 74.1 us -> 2.39 us  [the longest x1 1.19 us: on_device(): gathered[:, :own]]
    pallas_call x0 -> x9, Pallas kernels: none -> 66.3 us  [call(): pl.pallas_call(kernel, grid=grid, in_specs=in_specs, out_specs=out_specs,...]
  transfers between devices with their start and end apart: 9 -> 18, of which waited for: 6 -> 11; matrix products, arithmetic and copies ran while one was open for 2% -> 12% of each run, Pallas kernels for 0% -> 14%
where the time goes in v1:
time: 330 us; the launch traced here: 329 us
  waiting for transfers between devices  143 us (43%)
  Pallas kernels  66.3 us (20%)
  blocking collectives  41.2 us (12%)
  local copies, waits for them, and re-layouts  20.1 us (6%)
  other arithmetic  19.4 us (6%)
  matrix products  16.5 us (5%)
  between operations  15.5 us (5%)
  starting transfers between devices  7.1 us (2%)
    psum x1, waiting for transfers between devices, on_device(): lax.psum((query_weight_part, key_weight_part, value_weight_part, relative...  99.3 us
    pallas_call x9, Pallas kernels, call(): pl.pallas_call(kernel, grid=grid, in_specs=in_specs, out_specs=out_specs,...  66.3 us
    psum x1, blocking collectives, on_device(): lax.psum((query_weight_part, key_weight_part, value_weight_part, relative...  41.2 us
    ppermute x6, waiting for transfers between devices, swap_x(): return lax.ppermute(x, 'head', x_perm)  29.1 us
    all_gather x1, waiting for transfers between devices, on_device(): lax.all_gather(jnp.concatenate([content[0], query_stream[0], memory[0]],...  9.44 us
    unnamed x105, local copies, waits for them, and re-layouts  8.6 us
    dot_general x5, matrix products, dot_tn(): lax.dot_general(a, b, (((0,), (0,)), ((), ())), preferred_element_type=F32)  8.45 us
  transfers between devices with their start and end apart: 18, of which 11 were waited for; matrix products, arithmetic and copies ran while one was open for 12% of the time, Pallas kernels for 14%

profile of v1, /device:TPU:0, one launch (start us, length us, event | category | flops | bytes accessed | tf_op | source)
XLA Modules:
  0.0 329.5 jit_solution(14320438028294151660)
XLA Ops:
  7.3 1.9 pad_maximum_fusion.2
  9.3 3.0 collective-permute-start.4
  13.0 0.9 select_reduce_fusion
  13.9 1.1 copy.109
  17.4 1.0 fusion.6.wkv_ref
  18.4 1.1 select_convert_fusion.keycol_ref
  19.5 3.4 %fusion.rel_ref = bf16[1408,256]{1,0:T(8,128)(2,1)} fusion(bf16[1408,768]{1,0:T(8,128)(2,1)} %constant.61.clone, bf16[768,192]{0,1:T(8,128)(2,1)S(1)} %copy-done.43), kind=kOutput, calls=%fused_computation.1 | convolution fusion | flops 554008576 | bytes 3178496 | tf_op jit(solution)/shard_map/dot_general | solution.py:491
  22.9 9.4 %all-gather.3.cloned.1.call-done = bf16[992,768]{1,0:T(8,128)(2,1)} async-done(((bf16[248,768]{1,0:T(8,128)(2,1)}), bf16[992,768]{1,0:T(8,128)(2,1)}) %all-gather.3.cloned.1.call-update) | async-done | bytes 1523728 | tf_op jit(solution)/shard_map/all_gather | solution.py:429
  32.4 1.1 fusion.19
  33.4 1.2 slice.350
  34.8 1.3 pad_maximum_fusion.joined_ref
  36.3 21.5 %attend_forward.1 = (bf16[3,608,896]{2,1,0:T(8,128)(2,1)}, bf16[608,192]{1,0:T(8,128)(2,1)S(1)}, f32[608,256]{1,0:T(8,128)}, bf16[896,256]{1,0:T(8,128)(2,1)S(1)}, bf16[896,256]{1,0:T(8,128)(2,1)}) custom-call(bf16[608,768]{1,0:T(8,128)(2,1)} %copy-done.3, bf16[896,768]{1,0:T(8,128)(2,1)} %pad_maximum_fusion.joined_ref, bf16[768,256]{1,0:T(8,128)(2,1)S(1)} %pad.25.wq_ref, ...), custom_call_target="tpu_custom_call" | custom-call | tf_op jit(solution)/shard_map/attend_forward/pallas_call | solution.py:44
  59.5 8.7 %collective-permute-done.1.a2_ref = bf16[608,192]{1,0:T(8,128)(2,1)} collective-permute-done((bf16[608,192]{1,0:T(8,128)(2,1)S(1)}, bf16[608,192]{1,0:T(8,128)(2,1)}, u32[]{:S(2)}, u32[]{:S(2)}) %collective-permute-start.1) | collective-permute-done | bytes 233504 | tf_op jit(solution)/shard_map/ppermute | solution.py:417
  68.4 1.7 collective-permute-done.2.a3_ref
  70.2 7.8 %feed_forward.1 = (bf16[608,768]{1,0:T(8,128)(2,1)}, bf16[608,768]{1,0:T(8,128)(2,1)}, bf16[608,768]{1,0:T(8,128)(2,1)}, f32[304,768]{1,0:T(8,128)}, bf16[304,768]{1,0:T(8,128)(2,1)}, /*index=5*/bf16[304,768]{1,0:T(8,128)(2,1)}) custom-call(s32[1]{0:T(128)} %bitcast.core_ref, bf16[608,192]{1,0:T(8,128)(2,1)S(1)} %get-tuple-element.49.a0_ref, ...), custom_call_target="tpu_custom_call" | custom-call | tf_op jit(solution)/shard_map/feed_forward/pallas_call | solution.py:44
  80.1 1.0 copy-done
  81.2 1.0 collective-permute-start.7
  82.2 5.5 %collective-permute-done.8 = bf16[152,768]{1,0:T(8,128)(2,1)} collective-permute-done((bf16[152,768]{1,0:T(8,128)(2,1)}, bf16[152,768]{1,0:T(8,128)(2,1)}, u32[]{:S(2)}, u32[]{:S(2)}) %collective-permute-start.8) | collective-permute-done | bytes 233504 | tf_op jit(solution)/shard_map/ppermute | solution.py:417
  87.7 1.0 broadcast_select_fusion.4
  89.6 2.2 copy.116
  91.8 5.3 %collective-permute-done.7.b_ref = bf16[304,768]{1,0:T(8,128)(2,1)S(1)} collective-permute-done((bf16[304,768]{1,0:T(8,128)(2,1)S(1)}, bf16[304,768]{1,0:T(8,128)(2,1)S(1)}, u32[]{:S(2)}, u32[]{:S(2)}) %collective-permute-start.7) | collective-permute-done | bytes 466976 | tf_op jit(solution)/shard_map/ppermute | solution.py:417
  97.1 3.5 %second_norm.1 = (bf16[304,768]{1,0:T(8,128)(2,1)S(1)}, bf16[304,768]{1,0:T(8,128)(2,1)S(1)}, f32[304,768]{1,0:T(8,128)}, f32[8,768]{1,0:T(8,128)S(1)}) custom-call(bf16[304,768]{1,0:T(8,128)(2,1)S(1)} %add.93.a_ref, bf16[304,768]{1,0:T(8,128)(2,1)S(1)} %collective-permute-done.7.b_ref, f32[304,768]{1,0:T(8,128)} %get-tuple-element.52.mixed_ref, ...), custom_call_target="tpu_custom_call" | custom-call | tf_op jit(solution)/shard_map/second_norm/pallas_call | solution.py:44
  100.5 0.8 slice_bitcast_fusion.qft_ref
  101.4 1.0 collective-permute-done.9.other_ref
  102.3 4.3 %feed_backward.1 = (bf16[608,768]{1,0:T(8,128)(2,1)}, bf16[608,768]{1,0:T(8,128)(2,1)}, bf16[304,768]{1,0:T(8,128)(2,1)S(1)}, bf16[304,768]{1,0:T(8,128)(2,1)S(1)}, f32[8,768]{1,0:T(8,128)S(1)}) custom-call(s32[1]{0:T(128)} %bitcast.core_ref, bf16[304,768]{1,0:T(8,128)(2,1)S(1)} %get-tuple-element.54.mine_ref, ...), custom_call_target="tpu_custom_call" | custom-call | tf_op jit(solution)/shard_map/feed_backward/pallas_call | solution.py:44
  107.5 0.9 collective-permute-done.10.b_ref
  109.6 2.1 convolution_convert_fusion.2
  111.7 9.7 %collective-permute-done.11.b_ref = bf16[304,768]{1,0:T(8,128)(2,1)S(1)} collective-permute-done((bf16[304,768]{1,0:T(8,128)(2,1)S(1)}, bf16[304,768]{1,0:T(8,128)(2,1)S(1)}, u32[]{:S(2)}, u32[]{:S(2)}) %collective-permute-start.11) | collective-permute-done | bytes 466976 | tf_op jit(solution)/shard_map/ppermute | solution.py:417
  121.4 3.1 first_norm.1
  124.5 2.2 convolution_convert_fusion.1
  128.6 25.8 %attend_backward.1 = (bf16[608,192]{1,0:T(8,128)(2,1)S(1)}, bf16[192,896]{1,0:T(8,128)(2,1)S(1)}, bf16[192,896]{1,0:T(8,128)(2,1)S(1)}, bf16[192,1408]{1,0:T(8,128)(2,1)}, f32[8,256]{1,0:T(8,128)S(1)}) custom-call(bf16[3,608,896]{2,1,0:T(8,128)(2,1)} %get-tuple-element.60.p_ref, bf16[192,608]{1,0:T(8,128)(2,1)S(1)} %copy.118.dat_ref, ...), custom_call_target="tpu_custom_call" | custom-call | tf_op jit(solution)/shard_map/attend_backward/pallas_call | solution.py:44
  154.3 1.2 fusion.4
  155.6 1.2 fusion.5
  156.8 1.2 convolution_convert_fusion.8
  158.0 1.3 fusion.3
  159.3 1.7 fusion.7
  161.1 1.2 convolution_convert_fusion.5
  162.3 1.4 copy-done.5
  165.9 1.1 collective-permute-done.13.b_ref
  167.6 41.2 %all-reduce.8 = (f32[5,192]{1,0:T(8,128)S(1)}, f32[5,768]{1,0:T(8,128)S(1)}, f32[768]{0:T(1024)}) all-reduce(f32[5,192]{1,0:T(8,128)S(1)} %bitcast.94, f32[5,768]{1,0:T(8,128)S(1)} %fusion.38, f32[768]{0:T(1024)S(1)} %slice_reduce_fusion.5), channel_id=1, replica_groups=mesh['head'=4,'batch'=8] {'batch'}, use_global_device_ids=true, to_apply=%region_7.8 | all-reduce | flops 5568 | bytes 44544 | tf_op jit(solution)/shard_map/psum | solution.py:578
  213.7 99.3 %all-reduce.12.cloned.1.call-done = (bf16[768,192]{0,1:T(8,128)(2,1)}, bf16[768,192]{0,1:T(8,128)(2,1)}, bf16[768,192]{0,1:T(8,128)(2,1)}, bf16[192,768]{1,0:T(8...) async-done(((bf16[768,192]{0,1:T(8,128)(2,1)}, bf16[768,192]{0,1:T(8,128)(2,1)}, bf16[768,192]{0,1:T(8,128)(2,1)}, ...) | async-done | bytes 3833872 | tf_op jit(solution)/shard_map/psum | solution.py:578
  313.0 1.9 convert_element_type.93
  314.9 1.9 transpose.50
  316.8 0.9 transpose.52
  317.7 0.9 convert_element_type.97
  318.6 0.9 transpose.54
  319.4 1.6 convert_element_type.100
  321.1 1.6 convert_element_type.102
  (208 shorter events, 19.1 us)
Async XLA Ops:
  7.2 9.6 %copy-start.25 = (s32[1,512]{1,0:T(1,128)S(1)}, s32[1,512]{1,0:T(1,128)}, u32[]{:S(2)}) copy-start(s32[1,512]{1,0:T(1,128)} %param.31) | copy-start | bytes 6148
  7.2 8.4 %copy-start.24 = (s32[1,512]{1,0:T(1,128)S(1)}, s32[1,512]{1,0:T(1,128)}, u32[]{:S(2)}) copy-start(s32[1,512]{1,0:T(1,128)} %param.33) | copy-start | bytes 6148
  7.2 8.4 %copy-start.36 = (s32[1,96]{1,0:T(1,128)S(1)}, s32[1,96]{1,0:T(1,128)}, u32[]{:S(2)}) copy-start(s32[1,96]{1,0:T(1,128)} %param.32) | copy-start | bytes 1156
  7.2 7.8 %copy-start.13 = (bf16[768,192]{0,1:T(8,128)(2,1)S(1)}, bf16[768,192]{0,1:T(8,128)(2,1)}, u32[]{:S(2)}) copy-start(bf16[768,192]{0,1:T(8,128)(2,1)} %param.36) | copy-start | bytes 884740
  7.2 8.0 %copy-start.14 = (bf16[768,192]{0,1:T(8,128)(2,1)S(1)}, bf16[768,192]{0,1:T(8,128)(2,1)}, u32[]{:S(2)}) copy-start(bf16[768,192]{0,1:T(8,128)(2,1)} %param.35) | copy-start | bytes 884740
  7.3 9.5 %copy-start.33 = (bf16[3,64]{1,0:T(4,128)(2,1)S(1)}, bf16[3,64]{1,0:T(4,128)(2,1)}, u32[]{:S(2)}) copy-start(bf16[3,64]{1,0:T(4,128)(2,1)} %param.41) | copy-start | bytes 1156
  7.3 9.6 %copy-start.34 = (bf16[3,64]{1,0:T(4,128)(2,1)S(1)}, bf16[3,64]{1,0:T(4,128)(2,1)}, u32[]{:S(2)}) copy-start(bf16[3,64]{1,0:T(4,128)(2,1)} %param.40) | copy-start | bytes 1156
  7.3 9.7 %copy-start.35 = (bf16[3,64]{1,0:T(4,128)(2,1)S(1)}, bf16[3,64]{1,0:T(4,128)(2,1)}, u32[]{:S(2)}) copy-start(bf16[3,64]{1,0:T(4,128)(2,1)} %param.39) | copy-start | bytes 1156
  7.3 25.1 %all-gather.3.cloned.1.call-start = ((), (), s32[]{:S(2)}) async-start(), calls=%async_computation | async-start | bytes 1904640 | tf_op jit(solution)/shard_map/all_gather | solution.py:429
  7.3 9.7 %copy-start.32 = (bf16[2,3,64]{2,0,1:T(2,128)(2,1)S(1)}, bf16[2,3,64]{2,0,1:T(2,128)(2,1)}, u32[]{:S(2)}) copy-start(bf16[2,3,64]{2,0,1:T(2,128)(2,1)} %param.42) | copy-start | bytes 2308
  9.2 303.8 %all-reduce.12.cloned.1.call-start = ((), (), s32[]{:S(2)}) async-start(), calls=%async_computation.1 | async-start | bytes 7667712 | tf_op jit(solution)/shard_map/psum | solution.py:578
  9.3 49.7 %collective-permute-start.4 = (bf16[192,768]{1,0:T(8,128)(2,1)}, bf16[192,768]{1,0:T(8,128)(2,1)S(1)}, u32[]{:S(2)}, u32[]{:S(2)}) collective-permute-start(bf16[192,768]{1,0:T(8,128)(2,1)} %w0_ref.1), channel_id=1, source_target_pairs={{0,16},{8,24},{16,0},{24,8},{1,17},{9,25},{17,1},{25,9},{2,18},{10... | collective-permute-start | bytes 884744 | tf_op jit(solution)/shard_map/ppermute | solution.py:417
  16.0 3.5 %copy-start.43 = (bf16[768,192]{0,1:T(8,128)(2,1)S(1)}, bf16[768,192]{0,1:T(8,128)(2,1)}, u32[]{:S(2)}) copy-start(bf16[768,192]{0,1:T(8,128)(2,1)} %param.38) | copy-start | bytes 884740
  36.3 22.6 %copy-start.2 = (bf16[192,768]{1,0:T(8,128)(2,1)S(1)}, bf16[192,768]{1,0:T(8,128)(2,1)}, u32[]{:S(2)}) copy-start(bf16[192,768]{1,0:T(8,128)(2,1)} %w0_ref.1) | copy-start | bytes 884740
  36.3 31.9 %copy-start.26 = (bf16[768]{0:T(1024)(128)(2,1)S(1)}, bf16[768]{0:T(1024)(128)(2,1)}, u32[]{:S(2)}) copy-start(bf16[768]{0:T(1024)(128)(2,1)} %param.43) | copy-start | bytes 4612
  36.3 31.9 %copy-start.27 = (bf16[768]{0:T(1024)(128)(2,1)S(1)}, bf16[768]{0:T(1024)(128)(2,1)}, u32[]{:S(2)}) copy-start(bf16[768]{0:T(1024)(128)(2,1)} %param.44) | copy-start | bytes 4612
  36.3 32.0 %copy-start.28 = (bf16[768]{0:T(1024)(128)(2,1)S(1)}, bf16[768]{0:T(1024)(128)(2,1)}, u32[]{:S(2)}) copy-start(bf16[768]{0:T(1024)(128)(2,1)} %param.48) | copy-start | bytes 4612
  36.3 32.0 %copy-start.29 = (bf16[768]{0:T(1024)(128)(2,1)S(1)}, bf16[768]{0:T(1024)(128)(2,1)}, u32[]{:S(2)}) copy-start(bf16[768]{0:T(1024)(128)(2,1)} %param.49) | copy-start | bytes 4612
  36.3 32.0 %copy-start.30 = (bf16[768]{0:T(1024)(128)(2,1)S(1)}, bf16[768]{0:T(1024)(128)(2,1)}, u32[]{:S(2)}) copy-start(bf16[768]{0:T(1024)(128)(2,1)} %param.50) | copy-start | bytes 4612
  36.3 33.8 %copy-start.31 = (bf16[768]{0:T(1024)(128)(2,1)S(1)}, bf16[768]{0:T(1024)(128)(2,1)}, u32[]{:S(2)}) copy-start(bf16[768]{0:T(1024)(128)(2,1)} %param.46) | copy-start | bytes 4612
  58.6 9.6 %collective-permute-start.1 = (bf16[608,192]{1,0:T(8,128)(2,1)S(1)}, bf16[608,192]{1,0:T(8,128)(2,1)}, u32[]{:S(2)}, u32[]{:S(2)}) collective-permute-start(bf16[608,192]{1,0:T(8,128)(2,1)S(1)} %get-tuple-element.49.a0_ref), channel_id=1, source_target_pairs={{0,16},{8,24},{16,0},{24,8},{1,17},{9,25},{17,1},{25,9},{2,18},{10... | collective-permute-start | bytes 700424 | tf_op jit(solution)/shard_map/ppermute | solution.py:417
  58.9 9.5 %collective-permute-start.3 = (bf16[192,768]{1,0:T(8,128)(2,1)S(1)}, bf16[192,768]{1,0:T(8,128)(2,1)S(1)}, u32[]{:S(2)}, u32[]{:S(2)}) collective-permute-start(bf16[192,768]{1,0:T(8,128)(2,1)S(1)} %copy-done.2), channel_id=1, source_target_pairs={{0,8},{8,0},{16,24},{24,16},{1,9},{9,1},{17,25},{25,17},{2,10},{10... | collective-permute-start | bytes 884744 | tf_op jit(solution)/shard_map/ppermute | solution.py:414
  58.9 9.5 %collective-permute-start.5 = (bf16[192,768]{1,0:T(8,128)(2,1)S(1)}, bf16[192,768]{1,0:T(8,128)(2,1)S(1)}, u32[]{:S(2)}, u32[]{:S(2)}) collective-permute-start(bf16[192,768]{1,0:T(8,128)(2,1)S(1)} %collective-permute-done.4.w2_ref), channel_id=1, source_target_pairs={{0,8},{8,0},{16,24},{24,16},{1,9},{9,1},{17,25},{25,17},{2,10},{10... | collective-permute-start | bytes 884744 | tf_op jit(solution)/shard_map/ppermute | solution.py:414
  59.4 9.0 %collective-permute-start = (bf16[608,192]{1,0:T(8,128)(2,1)S(1)}, bf16[608,192]{1,0:T(8,128)(2,1)S(1)}, u32[]{:S(2)}, u32[]{:S(2)}) collective-permute-start(bf16[608,192]{1,0:T(8,128)(2,1)S(1)} %get-tuple-element.49.a0_ref), channel_id=1, source_target_pairs={{0,8},{8,0},{16,24},{24,16},{1,9},{9,1},{17,25},{25,17},{2,10},{10... | collective-permute-start | bytes 700424 | tf_op jit(solution)/shard_map/ppermute | solution.py:414
  68.2 1.9 collective-permute-start.2
  70.2 8.0 %copy-start.18 = (bf16[1,128,768]{2,1,0:T(8,128)(2,1)S(1)}, bf16[1,128,768]{2,1,0:T(8,128)(2,1)}, u32[]{:S(2)}) copy-start(bf16[1,128,768]{2,1,0:T(8,128)(2,1)} %param.51) | copy-start | bytes 589828
  70.2 8.0 %copy-start.23 = (bf16[1,24,768]{2,1,0:T(8,128)(2,1)S(1)}, bf16[1,24,768]{2,1,0:T(8,128)(2,1)}, u32[]{:S(2)}) copy-start(bf16[1,24,768]{2,1,0:T(8,128)(2,1)} %param.52) | copy-start | bytes 110596
  78.0 2.0 collective-permute-start.6
  78.9 8.8 %collective-permute-start.8 = (bf16[152,768]{1,0:T(8,128)(2,1)}, bf16[152,768]{1,0:T(8,128)(2,1)}, u32[]{:S(2)}, u32[]{:S(2)}) collective-permute-start(bf16[152,768]{1,0:T(8,128)(2,1)} %pad_maximum_fusion.4), channel_id=1, source_target_pairs={{0,16},{8,24},{16,0},{24,8},{1,17},{9,25},{17,1},{25,9},{2,18},{10... | collective-permute-start | bytes 700424 | tf_op jit(solution)/shard_map/ppermute | solution.py:417
  81.2 15.9 %collective-permute-start.7 = (bf16[304,768]{1,0:T(8,128)(2,1)S(1)}, bf16[304,768]{1,0:T(8,128)(2,1)S(1)}, u32[]{:S(2)}, u32[]{:S(2)}) collective-permute-start(bf16[304,768]{1,0:T(8,128)(2,1)S(1)} %add.93.a_ref), channel_id=1, source_target_pairs={{0,16},{8,24},{16,0},{24,8},{1,17},{9,25},{17,1},{25,9},{2,18},{10... | collective-permute-start | bytes 1400840 | tf_op jit(solution)/shard_map/ppermute | solution.py:417
  91.8 8.7 %copy-start.10 = (f32[608,256]{0,1:T(8,128)S(1)}, f32[608,256]{0,1:T(8,128)}, u32[]{:S(2)}) copy-start(f32[608,256]{0,1:T(8,128)} %copy.116) | copy-start | bytes 1867780
  100.5 1.8 collective-permute-start.9
  106.6 3.0 copy-start.38
  106.6 3.0 copy-start.40
  106.6 1.8 collective-permute-start.10
  108.6 12.8 %collective-permute-start.11 = (bf16[304,768]{1,0:T(8,128)(2,1)S(1)}, bf16[304,768]{1,0:T(8,128)(2,1)S(1)}, u32[]{:S(2)}, u32[]{:S(2)}) collective-permute-start(bf16[304,768]{1,0:T(8,128)(2,1)S(1)} %add.94.a_ref), channel_id=1, source_target_pairs={{0,16},{8,24},{16,0},{24,8},{1,17},{9,25},{17,1},{25,9},{2,18},{10... | collective-permute-start | bytes 1400840 | tf_op jit(solution)/shard_map/ppermute | solution.py:417
  111.7 12.8 %copy-start.37 = (bf16[608,768]{1,0:T(8,128)(2,1)S(1)}, bf16[608,768]{1,0:T(8,128)(2,1)}, u32[]{:S(2)}) copy-start(bf16[608,768]{1,0:T(8,128)(2,1)} %get-tuple-element.75) | copy-start | bytes 2801668
  111.7 12.8 %copy-start.39 = (bf16[608,768]{1,0:T(8,128)(2,1)S(1)}, bf16[608,768]{1,0:T(8,128)(2,1)}, u32[]{:S(2)}) copy-start(bf16[608,768]{1,0:T(8,128)(2,1)} %get-tuple-element.76) | copy-start | bytes 2801668
  124.5 2.9 collective-permute-start.12
  126.8 40.8 %collective-permute-start.15 = (f32[5,768]{1,0:T(8,128)S(1)}, f32[5,768]{1,0:T(8,128)S(1)}, u32[]{:S(2)}, u32[]{:S(2)}) collective-permute-start(f32[5,768]{1,0:T(8,128)S(1)} %pad_maximum_fusion.7), channel_id=1, source_target_pairs={{0,8},{8,0},{16,24},{24,16},{1,9},{9,1},{17,25},{25,17},{2,10},{10... | collective-permute-start | bytes 46088 | tf_op jit(solution)/shard_map/ppermute | solution.py:414
  128.5 25.8 %copy-start.8 = (bf16[4,96,768]{2,1,0:T(8,128)(2,1)S(1)}, bf16[4,96,768]{2,1,0:T(8,128)(2,1)}, u32[]{:S(2)}) copy-start(bf16[4,96,768]{2,1,0:T(8,128)(2,1)} %copy-done.7) | copy-start | bytes 1769476
  155.6 2.4 copy-start.9
  165.1 1.9 collective-permute-start.13
  167.2 45.0 %collective-permute-start.14 = (bf16[152,768]{1,0:T(8,128)(2,1)S(1)}, bf16[152,768]{1,0:T(8,128)(2,1)S(1)}, u32[]{:S(2)}, u32[]{:S(2)}) collective-permute-start(bf16[152,768]{1,0:T(8,128)(2,1)S(1)} %broadcast_select_fusion.2), channel_id=1, source_target_pairs={{0,16},{8,24},{16,0},{24,8},{1,17},{9,25},{17,1},{25,9},{2,18},{10... | collective-permute-start | bytes 700424 | tf_op jit(solution)/shard_map/ppermute | solution.py:417
  313.0 3.8 %copy-start.22 = (bf16[768,192]{0,1:T(8,128)(2,1)S(1)}, bf16[768,192]{0,1:T(8,128)(2,1)}, u32[]{:S(2)}) copy-start(bf16[768,192]{0,1:T(8,128)(2,1)} %get-tuple-element.199) | copy-start | bytes 884740
  313.0 4.7 %copy-start.21 = (bf16[192,768]{1,0:T(8,128)(2,1)S(1)}, bf16[192,768]{1,0:T(8,128)(2,1)}, u32[]{:S(2)}) copy-start(bf16[192,768]{1,0:T(8,128)(2,1)} %get-tuple-element.200) | copy-start | bytes 884740
  313.0 5.5 %copy-start.20 = (bf16[768,192]{0,1:T(8,128)(2,1)S(1)}, bf16[768,192]{0,1:T(8,128)(2,1)}, u32[]{:S(2)}) copy-start(bf16[768,192]{0,1:T(8,128)(2,1)} %get-tuple-element.201) | copy-start | bytes 884740
  314.9 4.5 %copy-start.12 = (bf16[768,768]{1,0:T(8,128)(2,1)S(1)}, bf16[768,768]{1,0:T(8,128)(2,1)}, u32[]{:S(2)}) copy-start(bf16[768,768]{1,0:T(8,128)(2,1)} %get-tuple-element.202) | copy-start | bytes 3538948
  (14 other events, 19.7 us)
Sparse Core Ops, SparseCore 0:
  10.3 22.0 all-gather.2
  162.4 150.5 all-reduce.11
